TPU v7x, 128 devices: a whole 4x4x4 slice. The times are simulated.
128 devices in a mesh: dp: 16 (over y, x), expert: 8 (over z, core).
Axes of the slice: x: 4, y: 4, z: 4, core: 2. Of those that a mesh axis runs over, the one named last changes fastest.
Arguments:
- tokens: bfloat16 [16384, 1280], P(('dp', 'expert')), may hold values from -6 to 6
- cotangent: bfloat16 [16384, 1280], P(('dp', 'expert')), may hold values from -4 to 4
- gate_weights: float32 [16384, 2], P(('dp', 'expert')), may hold values from 0.1 to 1
- expert_ids: int32 [16384, 2], P(('dp', 'expert')), may hold values from 0 to 15, as said below
- segments: int32 [128, 128], P(('dp', 'expert')), may hold values from 0 to 3, never falling along the last dimension, each value on 1 to 64 neighbouring positions
- keep_counts: int32 [128, 4], P(('dp', 'expert')), may hold values from 1 to 64
- expand_weight: bfloat16 [16, 2560, 1280], P('expert', 'dp'), may hold values from -0.15625 to 0.15625
- reduce_weight: bfloat16 [16, 2560, 1280], P('expert', 'dp'), may hold values from -0.125 to 0.125
Outputs:
- output: bfloat16 [16384, 1280], P(('dp', 'expert'))
- tokens_grad: bfloat16 [16384, 1280], P(('dp', 'expert'))
- gating_grad: float32 [16384, 2], P(('dp', 'expert'))
- expand_grad: bfloat16 [16, 2560, 1280], P('expert', 'dp')
- reduce_grad: bfloat16 [16, 2560, 1280], P('expert', 'dp')
Inputs may be any that keep to these rules, and one draw needn't show every extreme that they name: `expert_ids`: the 128 tokens of one sequence name each expert exactly 16 times, and a token's 2 experts differ. `segments`: within a sequence the ids never fall, every image 0 to 3 appears, each holds 1 to 64 positions.
All inputs are finite; a program needn't handle non-finite values.
Results may differ from a plain program's by a relative error of at most 0.015.
Values may be sent and summed in bfloat16 or wider, within the bound.
A program may use at most 128 MiB of HBM per device.

v0:
```python
import jax
import jax.numpy as jnp
from jax import lax
from jax.sharding import PartitionSpec as P

epsilon = 1e-06
root_half = 0.7071067811865476
density_scale = 0.3989422804014327


def gelu_value(values):
    return 0.5 * values * (1.0 + jax.scipy.special.erf(values * root_half))


def gelu_slope(values):
    return (
        0.5 * (1.0 + jax.scipy.special.erf(values * root_half))
        + values * jnp.exp(-0.5 * values * values) * density_scale
    )


def project_up(rows, weight):
    return jnp.einsum("rld,lhd->rlh", rows, weight, preferred_element_type=jnp.float32)


def project_down(hidden, weight):
    return jnp.einsum("rlh,lhd->rld", hidden, weight, preferred_element_type=jnp.float32)


def outer_rows(left, right):
    return jnp.einsum("rlh,rld->lhd", left, right, preferred_element_type=jnp.float32)


def body(
    tokens, cotangent, gate_weights, expert_ids, segments, keep_counts, expand_weight, reduce_weight
):
    tok_count = tokens.shape[0]
    top_count = expert_ids.shape[1]
    width = tokens.shape[1]
    sources = lax.axis_size("expert")
    local = expand_weight.shape[0]
    total_experts = local * sources
    pick_count = top_count * tok_count
    capacity = pick_count // total_experts
    image_ids = segments[0]
    position = jnp.arange(tok_count, dtype=jnp.int32)
    earlier_img = jnp.sum((image_ids[None, :] < image_ids[:, None]).astype(jnp.int32), axis=1)
    image_match = (
        image_ids[:, None] == jnp.arange(keep_counts.shape[1], dtype=jnp.int32)[None, :]
    ).astype(jnp.int32)
    keep_token = jnp.sum(image_match * keep_counts, axis=1)
    alive = (position - earlier_img < keep_token).astype(jnp.float32)
    tokens_wide = tokens.astype(jnp.float32)
    mean_rows = jnp.mean(tokens_wide, axis=1, keepdims=True)
    centred = tokens_wide - mean_rows
    inv_scale = lax.rsqrt(jnp.mean(centred * centred, axis=1, keepdims=True) + epsilon)
    normed = centred * inv_scale
    normed_low = normed.astype(jnp.bfloat16)
    choice_list = expert_ids.reshape(-1)
    matches = (choice_list[:, None] == jnp.arange(total_experts, dtype=jnp.int32)[None, :]).astype(
        jnp.int32
    )
    before = jnp.cumsum(matches, axis=0) - matches
    slot_list = jnp.sum(before * matches, axis=1)
    target = choice_list * capacity + slot_list
    order = (
        jnp.zeros((pick_count,), jnp.int32).at[target].set(jnp.arange(pick_count, dtype=jnp.int32))
    )
    source = order // top_count
    alive_pick = jnp.repeat(alive, top_count)
    weight_pick = gate_weights.reshape(-1) * alive_pick
    sent_rows = jnp.where(
        alive_pick[order][:, None] > 0, normed_low[source], jnp.zeros((), jnp.bfloat16)
    )
    cot_wide = cotangent.astype(jnp.float32)
    sent_grads = (cot_wide[source] * weight_pick[order][:, None]).astype(jnp.bfloat16)

    def to_slots(flat):
        return (
            flat.reshape(sources, local, capacity, width)
            .transpose(0, 2, 1, 3)
            .reshape(sources * capacity, local, width)
        )

    def from_slots(rows):
        return (
            rows.reshape(sources, capacity, local, width)
            .transpose(0, 2, 1, 3)
            .reshape(pick_count, width)
        )

    arrived = to_slots(lax.all_to_all(sent_rows, "expert", split_axis=0, concat_axis=0, tiled=True))
    arrived_grads = to_slots(
        lax.all_to_all(sent_grads, "expert", split_axis=0, concat_axis=0, tiled=True)
    )
    slot_rows = arrived.shape[0]
    all_rows = lax.all_gather(arrived, "dp", axis=0, tiled=True)
    pre = project_up(all_rows, expand_weight)
    hidden = gelu_value(pre).astype(jnp.bfloat16)
    results = lax.psum_scatter(
        project_down(hidden, reduce_weight).astype(jnp.bfloat16),
        "dp",
        scatter_dimension=0,
        tiled=True,
    )
    all_grads = lax.all_gather(arrived_grads, "dp", axis=0, tiled=True)
    back_hidden = project_up(all_grads, reduce_weight)
    dpre = (back_hidden * gelu_slope(pre)).astype(jnp.bfloat16)
    input_rows = lax.psum_scatter(
        project_down(dpre, expand_weight).astype(jnp.bfloat16),
        "dp",
        scatter_dimension=0,
        tiled=True,
    )

    def add_block(block, totals):
        offset = block * slot_rows
        hidden_block = lax.dynamic_slice_in_dim(hidden, offset, slot_rows, 0)
        dpre_block = lax.dynamic_slice_in_dim(dpre, offset, slot_rows, 0)
        grad_block = lax.dynamic_slice_in_dim(all_grads, offset, slot_rows, 0)
        row_block = lax.dynamic_slice_in_dim(all_rows, offset, slot_rows, 0)
        second_piece = lax.optimization_barrier(
            outer_rows(hidden_block, grad_block).astype(jnp.bfloat16)
        ).astype(jnp.float32)
        first_piece = lax.optimization_barrier(
            outer_rows(dpre_block, row_block).astype(jnp.bfloat16)
        ).astype(jnp.float32)
        return (totals[0] + first_piece, totals[1] + second_piece)

    empty = jnp.zeros(expand_weight.shape, jnp.float32)
    first_total, second_total = lax.fori_loop(
        0, all_rows.shape[0] // slot_rows, add_block, (empty, empty)
    )
    expand_grad = first_total.astype(jnp.bfloat16)
    reduce_grad = second_total.astype(jnp.bfloat16)
    returned = lax.all_to_all(
        from_slots(results), "expert", split_axis=0, concat_axis=0, tiled=True
    )
    result_pick = returned[target].astype(jnp.float32).reshape(tok_count, top_count, -1)
    output = (
        tokens_wide + jnp.sum(result_pick * weight_pick.reshape(tok_count, top_count, 1), axis=1)
    ).astype(jnp.bfloat16)
    gating_grad = alive_pick.reshape(tok_count, top_count) * jnp.sum(
        cot_wide[:, None, :] * result_pick, axis=2
    )
    returned_grads = lax.all_to_all(
        from_slots(input_rows), "expert", split_axis=0, concat_axis=0, tiled=True
    )
    input_pick = returned_grads[target].astype(jnp.float32).reshape(tok_count, top_count, -1)
    grad_norm = jnp.sum(input_pick * alive_pick.reshape(tok_count, top_count, 1), axis=1)
    tokens_grad = cot_wide + inv_scale * (
        grad_norm
        - jnp.mean(grad_norm, axis=1, keepdims=True)
        - normed * jnp.mean(grad_norm * normed, axis=1, keepdims=True)
    )
    return (output, tokens_grad.astype(jnp.bfloat16), gating_grad, expand_grad, reduce_grad)


def solution(mesh):
    in_specs = (
        P(("dp", "expert"), None),
        P(("dp", "expert"), None),
        P(("dp", "expert"), None),
        P(("dp", "expert"), None),
        P(("dp", "expert"), None),
        P(("dp", "expert"), None),
        P("expert", "dp", None),
        P("expert", "dp", None),
    )
    out_specs = (
        P(("dp", "expert"), None),
        P(("dp", "expert"), None),
        P(("dp", "expert"), None),
        P("expert", "dp", None),
        P("expert", "dp", None),
    )
    return jax.shard_map(body, mesh=mesh, in_specs=in_specs, out_specs=out_specs, check_vma=False)
```

profile of v0, /device:TPU:1, one launch (start us, length us, event | category | flops | bytes accessed | tf_op | source)
XLA Modules:
  0.0 434.9 jit_solution(15564184737724795476)
XLA Ops:
  16.0 1.9 gather_fusion
  19.6 17.6 %all_to_all.36 = bf16[8,32,1280]{2,1,0:T(8,128)(2,1)S(1)} all-to-all(bf16[8,32,1280]{2,1,0:T(8,128)(2,1)S(1)} %broadcast_select_fusion), channel_id=1, replica_groups=mesh['dp'=16,'expert'=8] {'expert'}, dimensions={0} | all-to-all | bytes 1310720 | tf_op jit(solution)/shard_map/all_to_all | solution.py:92
  38.4 1.9 gather_fusion.4
  41.9 14.2 %all_to_all.37 = bf16[8,32,1280]{2,1,0:T(8,128)(2,1)S(1)} all-to-all(bf16[8,32,1280]{2,1,0:T(8,128)(2,1)S(1)} %multiply_convert_fusion.1), channel_id=1, replica_groups=mesh['dp'=16,'expert'=8] {'expert'}, dimensions={0} | all-to-all | bytes 1310720 | tf_op jit(solution)/shard_map/all_to_all | solution.py:94
  57.1 61.1 %all-gather.3.cloned.1.call-done = bf16[2048,2,1280]{2,0,1:T(8,128)(2,1)} async-done(((bf16[128,2,1280]{2,0,1:T(8,128)(2,1)}), bf16[2048,2,1280]{2,0,1:T(8,128)(2,1)}) %all-gather.3.cloned.1.call-update) | async-done | bytes 10485776 | tf_op jit(solution)/shard_map/all_gather | solution.py:97
  118.2 9.1 %multiply_convert_fusion = (bf16[2048,2,160]{0,2,1:T(8,128)(2,1)S(1)}, f32[2048,2,160]{0,2,1:T(8,128)}) fusion(bf16[2048,2,1280]{2,0,1:T(8,128)(2,1)} %all-gather.3.cloned.1.call-done, bf16[2,160,1280]{2,1,0:T(8,128)(2,1)S(1)} %copy-done), kind=kOutput, calls=%fused_computation.30 | convolution fusion | flops 1680998400 | bytes 15237120 | tf_op jit(solution)/shard_map/rld,lhd->rlh/dot_general | solution.py:23
  127.3 73.6 %all-gather.5.cloned.1.call-done = bf16[2048,2,1280]{2,0,1:T(8,128)(2,1)} async-done(((bf16[128,2,1280]{2,0,1:T(8,128)(2,1)}), bf16[2048,2,1280]{2,0,1:T(8,128)(2,1)}) %all-gather.5.cloned.1.call-update) | async-done | bytes 10485776 | tf_op jit(solution)/shard_map/all_gather | solution.py:106
  200.9 8.6 %fusion.9 = bf16[2048,2,160]{0,2,1:T(8,128)(2,1)S(1)} fusion(bf16[2048,2,1280]{2,0,1:T(8,128)(2,1)} %all-gather.5.cloned.1.call-done, bf16[2,160,1280]{2,1,0:T(8,128)(2,1)} %param.17, f32[2048,2,160]{0,2,1:T(8,128)} %get-tuple-element.189), kind=kOutput, calls=%fused_computation.25 | convolution fusion | flops 1684275200 | bytes 15237120 | tf_op jit(solution)/shard_map/rld,lhd->rlh/dot_general | solution.py:23
  210.6 5.6 %fusion.7 = bf16[2048,2,1280]{2,0,1:T(8,128)(2,1)} fusion(bf16[2048,2,160]{0,2,1:T(8,128)(2,1)S(1)} %fusion.9, bf16[2,160,1280]{2,1,0:T(8,128)(2,1)S(1)} %copy-done), kind=kOutput, calls=%fused_computation.20 | convolution fusion | flops 1682964480 | bytes 12615680 | tf_op jit(solution)/shard_map/rlh,lhd->rld/dot_general | solution.py:27
  217.3 5.7 %fusion.6 = bf16[2048,2,1280]{2,0,1:T(8,128)(2,1)} fusion(bf16[2048,2,160]{0,2,1:T(8,128)(2,1)S(1)} %get-tuple-element.244, bf16[2,160,1280]{2,1,0:T(8,128)(2,1)S(1)} %copy-done.10), kind=kOutput, calls=%fused_computation.19 | convolution fusion | flops 1682964480 | bytes 12615680 | tf_op jit(solution)/shard_map/rlh,lhd->rld/dot_general | solution.py:27
  223.1 81.8 %reduce-scatter.5.cloned.1.call-done = bf16[128,2,1280]{2,0,1:T(8,128)(2,1)} async-done(((bf16[2048,2,1280]{2,0,1:T(8,128)(2,1)}), bf16[128,2,1280]{2,0,1:T(8,128)(2,1)}) %reduce-scatter.5.cloned.1.call-update) | async-done | bytes 655376 | tf_op jit(solution)/shard_map/reduce_scatter | solution.py:109
  304.9 2.0 copy.47
  306.9 5.9 %all-to-all-start.3 = ((bf16[8,32,1280]{2,1,0:T(8,128)(2,1)}), bf16[8,32,1280]{2,1,0:T(8,128)(2,1)}, u32[]{:S(2)}, u32[]{:S(2)}) async-start(bf16[8,32,1280]{2,1,0:T(8,128)(2,1)} %bitcast.23), calls=%async_computation.5 | async-start | bytes 1310720 | tf_op jit(solution)/shard_map/all_to_all | solution.py:146
  312.8 86.8 %while.16 = (s32[]{:T(128)}, f32[2,160,1280]{2,1,0:T(8,128)}, f32[2,160,1280]{2,1,0:T(8,128)S(1)}, bf16[2048,2,160]{0,2,1:T(8,128)(2,1)}, bf16[2048,2,1280]{2,0,...) while((s32[]{:T(128)}, f32[2,160,1280]{2,1,0:T(8,128)}, ...), condition=%wide.region_17.18_spmd.clone, body=%wide.region_16.17_spmd.clone.sunk | while | flops 212992000 | bytes 24414436 | solution.py:131
  312.8 1.6 convolution_convert_fusion.6
  318.2 1.6 convolution_convert_fusion.6
  323.6 1.6 convolution_convert_fusion.6
  325.3 1.5 convolution_convert_fusion.7
  329.1 1.6 convolution_convert_fusion.6
  330.7 1.6 convolution_convert_fusion.7
  334.6 1.6 convolution_convert_fusion.6
  336.2 1.5 convolution_convert_fusion.7
  340.0 1.6 convolution_convert_fusion.6
  341.6 1.6 convolution_convert_fusion.7
  345.5 1.6 convolution_convert_fusion.6
  347.1 1.5 convolution_convert_fusion.7
  350.9 1.6 convolution_convert_fusion.6
  356.3 1.6 convolution_convert_fusion.6
  358.0 1.5 convolution_convert_fusion.7
  361.8 1.6 convolution_convert_fusion.6
  367.2 1.6 convolution_convert_fusion.6
  368.8 1.5 convolution_convert_fusion.7
  372.6 1.6 convolution_convert_fusion.6
  374.2 1.5 convolution_convert_fusion.7
  378.0 1.6 convolution_convert_fusion.6
  383.4 1.6 convolution_convert_fusion.6
  388.8 1.6 convolution_convert_fusion.6
  390.4 1.5 convolution_convert_fusion.7
  394.2 1.6 convolution_convert_fusion.6
  395.8 1.5 convolution_convert_fusion.7
  402.3 2.0 copy.42
  404.3 4.8 %all-to-all-start.1 = ((bf16[8,32,1280]{2,1,0:T(8,128)(2,1)}), bf16[8,32,1280]{2,1,0:T(8,128)(2,1)S(1)}, u32[]{:S(2)}, u32[]{:S(2)}) async-start(bf16[8,32,1280]{2,1,0:T(8,128)(2,1)} %bitcast.13), calls=%async_computation.2 | async-start | bytes 1310720 | tf_op jit(solution)/shard_map/all_to_all | solution.py:136
  409.1 2.9 gather_fusion.5
  412.4 1.7 reshape.174
  414.2 3.0 multiply_reduce_fusion.2
  417.6 2.5 all-to-all-done.1
  421.3 1.7 reshape.173
  423.0 3.5 multiply_reduce_fusion
  (173 shorter events, 68.1 us)
Async XLA Ops:
  7.2 111.0 %copy-start = (bf16[2,160,1280]{2,1,0:T(8,128)(2,1)S(1)}, bf16[2,160,1280]{2,1,0:T(8,128)(2,1)}, u32[]{:S(2)}) copy-start(bf16[2,160,1280]{2,1,0:T(8,128)(2,1)} %param.16) | copy-start | bytes 2457604
  7.2 10.8 %copy-start.5 = (bf16[128,1280]{1,0:T(8,128)(2,1)S(1)}, bf16[128,1280]{1,0:T(8,128)(2,1)}, u32[]{:S(2)}) copy-start(bf16[128,1280]{1,0:T(8,128)(2,1)} %param.10) | copy-start | bytes 983044
  7.2 111.0 %all-gather.3.cloned.1.call-start = ((), (), s32[]{:S(2)}) async-start(), calls=%async_computation.6 | async-start | bytes 11141120 | tf_op jit(solution)/shard_map/all_gather | solution.py:97
  19.6 18.5 %copy-start.11 = (f32[128,2]{0,1:T(2,128)S(1)}, f32[128,2]{0,1:T(2,128)}, u32[]{:S(2)}) copy-start(f32[128,2]{0,1:T(2,128)} %param.12) | copy-start | bytes 3076
  37.2 3.3 copy-start.8
  38.1 162.8 %all-gather.5.cloned.1.call-start = ((), (), s32[]{:S(2)}) async-start(), calls=%async_computation.8 | async-start | bytes 11141120 | tf_op jit(solution)/shard_map/all_gather | solution.py:106
  57.0 247.9 %reduce-scatter.5.cloned.1.call-start = ((), (), s32[]{:S(2)}) async-start(), calls=%async_computation.9 | async-start | bytes 11141120 | tf_op jit(solution)/shard_map/reduce_scatter | solution.py:109
  127.3 89.1 %copy-start.6 = (bf16[2048,2,160]{0,2,1:T(8,128)(2,1)}, bf16[2048,2,160]{0,2,1:T(8,128)(2,1)S(1)}, u32[]{:S(2)}) copy-start(bf16[2048,2,160]{0,2,1:T(8,128)(2,1)S(1)} %get-tuple-element.244) | copy-start | bytes 3932164
  209.5 1.1 copy-start.7
  216.1 1.1 copy-start.10
  216.2 186.2 %reduce-scatter.3.cloned.1.call-start = ((), (), s32[]{:S(2)}) async-start(), calls=%async_computation.7 | async-start | bytes 11141120 | tf_op jit(solution)/shard_map/reduce_scatter | solution.py:100
  306.9 97.5 %all-to-all-start.3 = ((bf16[8,32,1280]{2,1,0:T(8,128)(2,1)}), bf16[8,32,1280]{2,1,0:T(8,128)(2,1)}, u32[]{:S(2)}, u32[]{:S(2)}) async-start(bf16[8,32,1280]{2,1,0:T(8,128)(2,1)} %bitcast.23), calls=%async_computation.5 | async-start | bytes 1310720 | tf_op jit(solution)/shard_map/all_to_all | solution.py:146
  312.8 3.1 copy-start.2
  317.0 1.2 copy-start.3
  318.2 3.1 copy-start.2
  322.5 1.2 copy-start.3
  323.6 3.2 copy-start.2
  327.9 1.2 copy-start.3
  329.1 3.2 copy-start.2
  333.4 1.2 copy-start.3
  334.6 3.2 copy-start.2
  338.8 1.2 copy-start.3
  340.0 3.2 copy-start.2
  344.3 1.2 copy-start.3
  345.5 3.1 copy-start.2
  349.7 1.2 copy-start.3
  350.9 3.1 copy-start.2
  355.1 1.2 copy-start.3
  356.3 3.1 copy-start.2
  360.6 1.2 copy-start.3
  361.8 3.1 copy-start.2
  366.0 1.2 copy-start.3
  367.2 3.1 copy-start.2
  371.4 1.2 copy-start.3
  372.6 3.1 copy-start.2
  376.8 1.2 copy-start.3
  378.0 3.1 copy-start.2
  382.2 1.2 copy-start.3
  383.4 3.1 copy-start.2
  387.6 1.2 copy-start.3
  388.8 3.2 copy-start.2
  393.0 1.2 copy-start.3
  394.2 3.2 copy-start.2
  398.5 1.2 copy-start.3
  399.6 1.7 copy-start.4
  404.3 15.7 %all-to-all-start.1 = ((bf16[8,32,1280]{2,1,0:T(8,128)(2,1)}), bf16[8,32,1280]{2,1,0:T(8,128)(2,1)S(1)}, u32[]{:S(2)}, u32[]{:S(2)}) async-start(bf16[8,32,1280]{2,1,0:T(8,128)(2,1)} %bitcast.13), calls=%async_computation.2 | async-start | bytes 1310720 | tf_op jit(solution)/shard_map/all_to_all | solution.py:136
  423.0 4.2 copy-start.9
  423.0 5.4 %copy-start.1 = (bf16[2,160,1280]{2,1,0:T(8,128)(2,1)S(1)}, bf16[2,160,1280]{2,1,0:T(8,128)(2,1)}, u32[]{:S(2)}) copy-start(bf16[2,160,1280]{2,1,0:T(8,128)(2,1)} %param.16) | copy-start | bytes 2457604
Sparse Core Ops, SparseCore 0:
  38.2 79.9 all-gather.2
  120.9 79.9 all-gather.4
  216.3 88.5 reduce-scatter.4
  308.2 88.6 reduce-scatter.2
where the time goes:
time: 436 us; the launch traced here: 435 us
  waiting for transfers between devices  219 us (50%)
  matrix products  79 us (18%)
  local copies, waits for them, and re-layouts  45.8 us (11%)
  other arithmetic  33.5 us (8%)
  blocking collectives  31.8 us (7%)
  between operations  14 us (3%)
  starting transfers between devices  11.1 us (3%)
    reduce_scatter x1, waiting for transfers between devices, body(): lax.psum_scatter(project_down(dpre, expand_weight).astype(jnp.bfloat16),...  81.8 us
    all_gather x1, waiting for transfers between devices, body(): all_grads = lax.all_gather(arrived_grads, 'dp', axis=0, tiled=True)  73.6 us
    all_gather x1, waiting for transfers between devices, body(): all_rows = lax.all_gather(arrived, 'dp', axis=0, tiled=True)  61.1 us
    dot_general x32, matrix products, outer_rows(): jnp.einsum('rlh,rld->lhd', left, right, preferred_element_type=jnp.float32)  50.1 us
    while x64, local copies, waits for them, and re-layouts  19 us
    dot_general x2, matrix products, project_up(): jnp.einsum('rld,lhd->rlh', rows, weight, preferred_element_type=jnp.float32)  17.7 us
    all_to_all x1, blocking collectives, body(): lax.all_to_all(sent_rows, 'expert', split_axis=0, concat_axis=0, tiled=True)  17.6 us
    add x16, other arithmetic, add_block(): return (totals[0] + first_piece, totals[1] + second_piece)  17.2 us
  transfers between devices with their start and end apart: 6, of which 4 were waited for; matrix products, arithmetic and copies ran while one was open for 23% of the time, Pallas kernels for 0%

commit v1 on v0

--- a/solution.py
+++ b/solution.py
@@ -103,7 +103,15 @@
         scatter_dimension=0,
         tiled=True,
     )
-    all_grads = lax.all_gather(arrived_grads, "dp", axis=0, tiled=True)
+    all_grads = jnp.concatenate(
+        lax.all_to_all(
+            jnp.stack([arrived_grads for _ in range(lax.axis_size("dp"))], axis=0),
+            axis_name="dp",
+            split_axis=0,
+            concat_axis=0,
+        ),
+        axis=0,
+    )
     back_hidden = project_up(all_grads, reduce_weight)
     dpre = (back_hidden * gelu_slope(pre)).astype(jnp.bfloat16)
     input_rows = lax.psum_scatter(

time: 436 us -> 499 us (1.14)
  blocking collectives: 31.8 us -> 198 us
  waiting for transfers between devices: 219 us -> 81.3 us
  other arithmetic: 33.5 us -> 75.5 us
  local copies, waits for them, and re-layouts: 45.8 us -> 39.1 us
    all_to_all x0 -> x1, blocking collectives: none -> 166 us  [body(): lax.all_to_all(jnp.stack([arrived_grads for _ in range(lax.axis_size('dp'...]
    all_gather x1 -> x0, waiting for transfers between devices: 73.6 us -> none  [body(): all_grads = lax.all_gather(arrived_grads, 'dp', axis=0, tiled=True)]
    all_gather x1, waiting for transfers between devices: 61.1 us -> 0.01 us  [body(): all_rows = lax.all_gather(arrived, 'dp', axis=0, tiled=True)]
    add x16, other arithmetic: 17.2 us -> 58.2 us  [add_block(): return (totals[0] + first_piece, totals[1] + second_piece)]
    while x64 -> x0, local copies, waits for them, and re-layouts: 19 us -> none
    all_to_all x0 -> x1, local copies, waits for them, and re-layouts: none -> 8.94 us  [body(): lax.all_to_all(jnp.stack([arrived_grads for _ in range(lax.axis_size('dp'...]
    another operation x1 -> x2, local copies, waits for them, and re-layouts: 0.01 us -> 5.02 us  [the longest x1 5.02 us: body(): jnp.stack([arrived_grads for _ in range(lax.axis_size('dp'))], axis=0)]
  transfers between devices with their start and end apart: 6 -> 5, of which waited for: 4 -> 2; matrix products, arithmetic and copies ran while one was open for 23% -> 29% of each run, Pallas kernels for 0% -> 0%
where the time goes in v1:
time: 499 us; the launch traced here: 497 us
  blocking collectives  198 us (40%)
  waiting for transfers between devices  81.3 us (16%)
  matrix products  78.2 us (16%)
  other arithmetic  75.5 us (15%)
  local copies, waits for them, and re-layouts  39.1 us (8%)
  between operations  14 us (3%)
  starting transfers between devices  10.7 us (2%)
    all_to_all x1, blocking collectives, body(): lax.all_to_all(jnp.stack([arrived_grads for _ in range(lax.axis_size('dp'...  166 us
    reduce_scatter x1, waiting for transfers between devices, body(): lax.psum_scatter(project_down(dpre, expand_weight).astype(jnp.bfloat16),...  78.8 us
    add x16, other arithmetic, add_block(): return (totals[0] + first_piece, totals[1] + second_piece)  58.2 us
    dot_general x32, matrix products, outer_rows(): jnp.einsum('rlh,rld->lhd', left, right, preferred_element_type=jnp.float32)  48.7 us
    all_to_all x1, blocking collectives, body(): lax.all_to_all(sent_rows, 'expert', split_axis=0, concat_axis=0, tiled=True)  17.7 us
    dot_general x2, matrix products, project_up(): jnp.einsum('rld,lhd->rlh', rows, weight, preferred_element_type=jnp.float32)  15.6 us
    all_to_all x1, blocking collectives, body(): lax.all_to_all(sent_grads, 'expert', split_axis=0, concat_axis=0, tiled=T...  14.2 us
    dot_general x2, matrix products, project_down(): jnp.einsum('rlh,lhd->rld', hidden, weight, preferred_element_type=jnp.flo...  13.9 us
  transfers between devices with their start and end apart: 5, of which 2 were waited for; matrix products, arithmetic and copies ran while one was open for 29% of the time, Pallas kernels for 0%

profile of v1, /device:TPU:1, one launch (start us, length us, event | category | flops | bytes accessed | tf_op | source)
XLA Modules:
  0.0 497.2 jit_solution(322649769619000075)
XLA Ops:
  17.1 1.9 gather_fusion
  20.5 17.7 %all_to_all.41 = bf16[8,32,1280]{2,1,0:T(8,128)(2,1)S(1)} all-to-all(bf16[8,32,1280]{2,1,0:T(8,128)(2,1)S(1)} %broadcast_select_fusion), channel_id=1, replica_groups=mesh['dp'=16,'expert'=8] {'expert'}, dimensions={0} | all-to-all | bytes 1310720 | tf_op jit(solution)/shard_map/all_to_all | solution.py:92
  40.8 1.9 gather_fusion.4
  42.9 14.2 %all_to_all.42 = bf16[8,32,1280]{2,1,0:T(8,128)(2,1)S(1)} all-to-all(bf16[8,32,1280]{2,1,0:T(8,128)(2,1)S(1)} %multiply_convert_fusion.1), channel_id=1, replica_groups=mesh['dp'=16,'expert'=8] {'expert'}, dimensions={0} | all-to-all | bytes 1310720 | tf_op jit(solution)/shard_map/all_to_all | solution.py:94
  57.2 5.0 %stack.3 = bf16[16,128,2,1280]{3,1,2,0:T(8,128)(2,1)} broadcast(bf16[128,2,1280]{2,0,1:T(8,128)(2,1)S(1)} %bitcast.72), dimensions={1,2,3} | broadcast | bytes 11141120 | tf_op jit(solution)/shard_map/stack | solution.py:108
  62.2 166.1 %all_to_all.43 = bf16[16,128,2,1280]{3,1,2,0:T(8,128)(2,1)} all-to-all(bf16[16,128,2,1280]{3,1,2,0:T(8,128)(2,1)} %stack.3), channel_id=1, replica_groups=mesh['dp'=16,'expert'=8] {'dp'}, dimensions={0} | all-to-all | bytes 20971520 | tf_op jit(solution)/shard_map/all_to_all | solution.py:107
  228.4 8.9 %copy.49 = bf16[16,128,2,1280]{3,1,0,2:T(8,128)(2,1)} copy(bf16[16,128,2,1280]{3,1,2,0:T(8,128)(2,1)} %all_to_all.43) | data formatting | bytes 20971520 | tf_op jit(solution)/shard_map/all_to_all | solution.py:107
  237.3 6.3 %multiply_convert_fusion = (bf16[2048,2,160]{0,2,1:T(8,128)(2,1)S(1)}, f32[2048,2,160]{0,2,1:T(8,128)S(1)}) fusion(bf16[2048,2,1280]{2,0,1:T(8,128)(2,1)} %all-gather.2.cloned.1.call-done, bf16[2,160,1280]{2,1,0:T(8,128)(2,1)S(1)} %copy-done), kind=kOutput, calls=%fused_computation.30 | convolution fusion | flops 1680998400 | bytes 15237120 | tf_op jit(solution)/shard_map/rld,lhd->rlh/dot_general | solution.py:23
  243.6 9.3 %fusion.9 = bf16[2048,2,160]{0,2,1:T(8,128)(2,1)} fusion(bf16[2048,2,1280]{2,0,1:T(8,128)(2,1)} %bitcast.65, bf16[2,160,1280]{2,1,0:T(8,128)(2,1)} %param.17, f32[2048,2,160]{0,2,1:T(8,128)S(1)} %get-tuple-element.189), kind=kOutput, calls=%fused_computation.25 | convolution fusion | flops 1684275200 | bytes 15237120 | tf_op jit(solution)/shard_map/rld,lhd->rlh/dot_general | solution.py:23
  253.0 8.1 %fusion.7 = bf16[2048,2,1280]{2,0,1:T(8,128)(2,1)} fusion(bf16[2048,2,160]{0,2,1:T(8,128)(2,1)} %fusion.9, bf16[2,160,1280]{2,1,0:T(8,128)(2,1)S(1)} %copy-done), kind=kOutput, calls=%fused_computation.20 | convolution fusion | flops 1682964480 | bytes 12615680 | tf_op jit(solution)/shard_map/rlh,lhd->rld/dot_general | solution.py:27
  262.3 5.8 %fusion.6 = bf16[2048,2,1280]{2,0,1:T(8,128)(2,1)} fusion(bf16[2048,2,160]{0,2,1:T(8,128)(2,1)S(1)} %get-tuple-element.244, bf16[2,160,1280]{2,1,0:T(8,128)(2,1)S(1)} %copy-done.6), kind=kOutput, calls=%fused_computation.19 | convolution fusion | flops 1682964480 | bytes 12615680 | tf_op jit(solution)/shard_map/rlh,lhd->rld/dot_general | solution.py:27
  268.2 78.8 %reduce-scatter.5.cloned.1.call-done = bf16[128,2,1280]{2,0,1:T(8,128)(2,1)} async-done(((bf16[2048,2,1280]{2,0,1:T(8,128)(2,1)}), bf16[128,2,1280]{2,0,1:T(8,128)(2,1)}) %reduce-scatter.5.cloned.1.call-update) | async-done | bytes 655376 | tf_op jit(solution)/shard_map/reduce_scatter | solution.py:117
  347.0 2.0 copy.50
  348.9 6.0 %all-to-all-start.4 = ((bf16[8,32,1280]{2,1,0:T(8,128)(2,1)}), bf16[8,32,1280]{2,1,0:T(8,128)(2,1)}, u32[]{:S(2)}, u32[]{:S(2)}) async-start(bf16[8,32,1280]{2,1,0:T(8,128)(2,1)} %bitcast.24), calls=%async_computation.6 | async-start | bytes 1310720 | tf_op jit(solution)/shard_map/all_to_all | solution.py:154
  354.9 107.2 %while.16 = (s32[]{:T(128)}, f32[2,160,1280]{2,1,0:T(8,128)S(1)}, f32[2,160,1280]{2,1,0:T(8,128)}, bf16[2048,2,160]{0,2,1:T(8,128)(2,1)}, bf16[2048,2,1280]{2,0,...) while((s32[]{:T(128)}, f32[2,160,1280]{2,1,0:T(8,128)S(1)}, ...), condition=%wide.region_17.18_spmd.clone, body=%wide.region_16.17_spmd.clone.sunk | while | flops 212992000 | bytes 11307181 | solution.py:139
  357.9 2.3 select_add_fusion.3
  360.2 1.5 convolution_convert_fusion.6
  363.3 3.7 select_add_fusion.3
  370.0 3.7 select_add_fusion.3
  373.7 1.6 convolution_convert_fusion.6
  375.3 1.6 convolution_convert_fusion.7
  376.9 3.7 select_add_fusion.3
  383.7 3.8 select_add_fusion.3
  389.0 1.5 convolution_convert_fusion.7
  390.6 3.7 select_add_fusion.3
  395.8 1.6 convolution_convert_fusion.7
  397.5 3.8 select_add_fusion.3
  404.3 3.7 select_add_fusion.3
  409.6 1.5 convolution_convert_fusion.7
  411.1 3.7 select_add_fusion.3
  417.8 3.7 select_add_fusion.3
  423.0 1.7 convolution_convert_fusion.7
  424.8 3.7 select_add_fusion.3
  430.0 1.5 convolution_convert_fusion.7
  431.5 3.7 select_add_fusion.3
  436.7 1.5 convolution_convert_fusion.7
  438.3 3.7 select_add_fusion.3
  445.0 3.7 select_add_fusion.3
  451.7 3.7 select_add_fusion.3
  458.4 3.7 select_add_fusion.3
  464.8 2.0 copy.44
  466.9 4.6 all-to-all-start.1
  471.5 2.9 gather_fusion.5
  474.4 1.7 reshape.176
  476.4 3.0 multiply_reduce_fusion.2
  479.9 2.5 all-to-all-done.1
  483.6 1.7 reshape.175
  485.3 3.5 multiply_reduce_fusion
  (105 shorter events, 56.5 us)
Async XLA Ops:
  7.2 230.2 %copy-start = (bf16[2,160,1280]{2,1,0:T(8,128)(2,1)S(1)}, bf16[2,160,1280]{2,1,0:T(8,128)(2,1)}, u32[]{:S(2)}) copy-start(bf16[2,160,1280]{2,1,0:T(8,128)(2,1)} %param.16) | copy-start | bytes 2457604
  7.2 230.2 %all-gather.2.cloned.1.call-start = ((), (), s32[]{:S(2)}) async-start(), calls=%async_computation.7 | async-start | bytes 11141120 | tf_op jit(solution)/shard_map/all_gather | solution.py:97
  20.5 18.7 %copy-start.5 = (bf16[128,1280]{1,0:T(8,128)(2,1)S(1)}, bf16[128,1280]{1,0:T(8,128)(2,1)}, u32[]{:S(2)}) copy-start(bf16[128,1280]{1,0:T(8,128)(2,1)} %param.11) | copy-start | bytes 983044
  39.1 307.8 %reduce-scatter.5.cloned.1.call-start = ((), (), s32[]{:S(2)}) async-start(), calls=%async_computation.9 | async-start | bytes 11141120 | tf_op jit(solution)/shard_map/reduce_scatter | solution.py:117
  39.2 1.2 copy-start.7
  243.6 17.6 %copy-start.4 = (bf16[2048,2,160]{0,2,1:T(8,128)(2,1)}, bf16[2048,2,160]{0,2,1:T(8,128)(2,1)S(1)}, u32[]{:S(2)}) copy-start(bf16[2048,2,160]{0,2,1:T(8,128)(2,1)S(1)} %get-tuple-element.244) | copy-start | bytes 3932164
  261.1 1.1 copy-start.6
  261.1 203.7 %reduce-scatter.3.cloned.1.call-start = ((), (), s32[]{:S(2)}) async-start(), calls=%async_computation.8 | async-start | bytes 11141120 | tf_op jit(solution)/shard_map/reduce_scatter | solution.py:100
  348.9 117.9 %all-to-all-start.4 = ((bf16[8,32,1280]{2,1,0:T(8,128)(2,1)}), bf16[8,32,1280]{2,1,0:T(8,128)(2,1)}, u32[]{:S(2)}, u32[]{:S(2)}) async-start(bf16[8,32,1280]{2,1,0:T(8,128)(2,1)} %bitcast.24), calls=%async_computation.6 | async-start | bytes 1310720 | tf_op jit(solution)/shard_map/all_to_all | solution.py:154
  462.1 1.7 copy-start.2
  466.9 15.5 %all-to-all-start.1 = ((bf16[8,32,1280]{2,1,0:T(8,128)(2,1)}), bf16[8,32,1280]{2,1,0:T(8,128)(2,1)S(1)}, u32[]{:S(2)}, u32[]{:S(2)}) async-start(bf16[8,32,1280]{2,1,0:T(8,128)(2,1)} %bitcast.13), calls=%async_computation.2 | async-start | bytes 1310720 | tf_op jit(solution)/shard_map/all_to_all | solution.py:144
  476.1 3.5 copy-start.3
  485.3 5.4 %copy-start.1 = (bf16[2,160,1280]{2,1,0:T(8,128)(2,1)S(1)}, bf16[2,160,1280]{2,1,0:T(8,128)(2,1)}, u32[]{:S(2)}) copy-start(bf16[2,160,1280]{2,1,0:T(8,128)(2,1)} %param.16) | copy-start | bytes 2457604
Sparse Core Ops, SparseCore 0:
  39.3 183.9 all-gather.1
  261.3 85.6 reduce-scatter.4
  350.4 89.0 reduce-scatter.2
